TPU v7x, 256 devices: a whole 4x4x8 slice. The times are simulated.
256 devices in a mesh: sub: 64 (over z, y, core), blk: 4 (over x).
Axes of the slice: x: 4, y: 4, z: 8, core: 2. Of those that a mesh axis runs over, the one named last changes fastest.
Arguments:
- inputs: bfloat16 [16, 1048576], P(None, ('sub', 'blk')), may hold values from -6 to 6
- adjoint_in: bfloat16 [16, 1048576], P(None, ('sub', 'blk')), may hold values from -6 to 6
- panel_map: int32 [256, 4096], P(('sub', 'blk')), may hold values from 0 to 4095, each once within a row
- bases: bfloat16 [4096, 128, 256], P(('sub', 'blk')), may hold values from -0.375 to 0.375
- near_blocks: bfloat16 [4096, 256, 256], P(('sub', 'blk')), may hold values from -0.375 to 0.375
- transfers: bfloat16 [4096, 128, 128], P(('sub', 'blk')), may hold values from -0.125 to 0.125
- up_maps: bfloat16 [1536, 128, 128], P(('sub', 'blk')), may hold values from -0.5 to 0.5
- down_maps: bfloat16 [1536, 128, 128], P(('sub', 'blk')), may hold values from -0.5 to 0.5
- send_list: int32 [256, 128], P(('sub', 'blk')), may hold values from 0 to 15
- target_leaf: int32 [256, 128], P(('sub', 'blk')), may hold values from 0 to 15
- couplings: bfloat16 [32768, 128, 128], P(('sub', 'blk')), may hold values from -0.5 to 0.5
Outputs:
- product: bfloat16 [16, 1048576], P(None, ('sub', 'blk'))
- adjoint_product: bfloat16 [16, 1048576], P(None, ('sub', 'blk'))
Inputs may be any that keep to these rules, and one draw needn't show every extreme that they name: `panel_map`: each row is a permutation of 0 to 4095. `send_list`: entries name leaves of the sending group. `target_leaf`: entries name leaves of the receiving group.
All inputs are finite; a program needn't handle non-finite values.
Results may differ from a plain program's by a relative error of at most 0.0059.
Values may be sent and summed in bfloat16 or wider, within the bound.
A program may use at most 64 MiB of HBM per device.

v0:
```python
import jax
import jax.numpy as jnp
from jax import lax
from jax.sharding import PartitionSpec as P

HIGHEST = lax.Precision.HIGHEST


def leaf_onehot(indices, count):
    return (indices[:, None] == jnp.arange(count, dtype=jnp.int32)[None, :]).astype(jnp.float32)


def shards(
    inputs,
    adjoint_in,
    panel_map,
    bases,
    near_blocks,
    transfers,
    up_maps,
    down_maps,
    send_list,
    target_leaf,
    couplings,
):
    leaf_count = transfers.shape[0]
    rank_size = bases.shape[1]
    leaf_size = bases.shape[2]
    rhs_count = inputs.shape[0]
    ordering = panel_map[0]
    forward = jnp.take(inputs, ordering, axis=1).reshape(rhs_count, leaf_count, leaf_size)
    backward = jnp.take(adjoint_in, ordering, axis=1).reshape(rhs_count, leaf_count, leaf_size)
    fwd_skel = jnp.einsum(
        "mlp,lkp->lmk", forward, bases, preferred_element_type=jnp.float32
    ).astype(jnp.bfloat16)
    bwd_skel = jnp.einsum(
        "mlp,lkp->lmk", backward, bases, preferred_element_type=jnp.float32
    ).astype(jnp.bfloat16)
    fwd_group = jnp.einsum("lmk,ljk->mj", fwd_skel, transfers, preferred_element_type=jnp.float32)
    bwd_group = jnp.einsum("lmk,lkj->mj", bwd_skel, transfers, preferred_element_type=jnp.float32)
    up_float = up_maps.astype(jnp.float32)
    down_float = down_maps.astype(jnp.float32)
    fwd_terms = jnp.einsum("mj,lij->lmi", fwd_group, up_float, precision=HIGHEST)
    bwd_terms = jnp.einsum("mj,lji->lmi", bwd_group, down_float, precision=HIGHEST)
    fwd_terms, bwd_terms = lax.psum((fwd_terms, bwd_terms), "blk")
    levels = fwd_terms.shape[0]
    all_fwd, all_bwd = (
        lax.all_gather(fwd_terms, "sub", axis=0, tiled=True),
        lax.all_gather(bwd_terms, "sub", axis=0, tiled=True),
    )
    subtrees = all_fwd.shape[0] // levels
    all_fwd = all_fwd.reshape(subtrees, levels, rhs_count, rank_size)
    all_bwd = all_bwd.reshape(subtrees, levels, rhs_count, rank_size)
    own_index = lax.axis_index("sub")
    level_ids = jnp.arange(levels, dtype=jnp.int32)[:, None]
    peer_ids = jnp.arange(subtrees, dtype=jnp.int32)[None, :]
    partner = jnp.bitwise_xor(jnp.right_shift(own_index, level_ids), 1)
    weights = (jnp.right_shift(peer_ids, level_ids) == partner).astype(jnp.float32)
    sib_fwd = jnp.einsum("lr,rlmk->lmk", weights, all_fwd, precision=HIGHEST)
    sib_bwd = jnp.einsum("lr,rlmk->lmk", weights, all_bwd, precision=HIGHEST)
    fwd_local = jnp.einsum("lmi,lji->mj", sib_fwd, down_float, precision=HIGHEST)
    bwd_local = jnp.einsum("lmi,lij->mj", sib_bwd, up_float, precision=HIGHEST)
    send_rows = send_list[0]
    target_rows = target_leaf[0]
    outgoing = jnp.take(fwd_skel, send_rows, axis=0)
    picked = jnp.take(bwd_skel, target_rows, axis=0)
    incoming = lax.all_to_all(outgoing, "sub", split_axis=0, concat_axis=0, tiled=True)
    returned_src = jnp.einsum(
        "qmi,qik->qmk", picked, couplings, preferred_element_type=jnp.float32
    ).astype(jnp.bfloat16)
    returned = lax.all_to_all(returned_src, "sub", split_axis=0, concat_axis=0, tiled=True)
    list_terms = jnp.einsum("qmk,qik->qmi", incoming, couplings, preferred_element_type=jnp.float32)
    list_fwd = jnp.einsum(
        "ql,qmi->lmi", leaf_onehot(target_rows, leaf_count), list_terms, precision=HIGHEST
    )
    list_bwd = jnp.einsum(
        "ql,qmk->lmk",
        leaf_onehot(send_rows, leaf_count),
        returned.astype(jnp.float32),
        precision=HIGHEST,
    )
    near_fwd = jnp.einsum("mlq,lpq->mlp", forward, near_blocks, preferred_element_type=jnp.float32)
    near_bwd = jnp.einsum("mlp,lpq->mlq", backward, near_blocks, preferred_element_type=jnp.float32)
    transfer_float = transfers.astype(jnp.float32)
    fwd_leaf = (
        jnp.einsum("mj,ljk->lmk", fwd_local, transfer_float, precision=HIGHEST) + list_fwd
    ).astype(jnp.bfloat16)
    bwd_leaf = (
        jnp.einsum("mj,lkj->lmk", bwd_local, transfer_float, precision=HIGHEST) + list_bwd
    ).astype(jnp.bfloat16)
    fwd_vals = (
        jnp.einsum("lmk,lkp->mlp", fwd_leaf, bases, preferred_element_type=jnp.float32) + near_fwd
    )
    bwd_vals = (
        jnp.einsum("lmk,lkp->mlp", bwd_leaf, bases, preferred_element_type=jnp.float32) + near_bwd
    )
    fwd_vals = fwd_vals.reshape(rhs_count, leaf_count * leaf_size).astype(jnp.bfloat16)
    bwd_vals = bwd_vals.reshape(rhs_count, leaf_count * leaf_size).astype(jnp.bfloat16)
    product = jnp.zeros_like(inputs).at[:, ordering].set(fwd_vals)
    adjoint_product = jnp.zeros_like(adjoint_in).at[:, ordering].set(bwd_vals)
    return (product, adjoint_product)


def solution(mesh):
    return jax.shard_map(
        shards,
        mesh=mesh,
        in_specs=(
            P(None, ("sub", "blk")),
            P(None, ("sub", "blk")),
            P(("sub", "blk"), None),
            P(("sub", "blk"), None, None),
            P(("sub", "blk"), None, None),
            P(("sub", "blk"), None, None),
            P(("sub", "blk"), None, None),
            P(("sub", "blk"), None, None),
            P(("sub", "blk"), None),
            P(("sub", "blk"), None),
            P(("sub", "blk"), None, None),
        ),
        out_specs=(P(None, ("sub", "blk")), P(None, ("sub", "blk"))),
        check_vma=False,
    )
```

profile of v0, /device:TPU:1, one launch (start us, length us, event | category | flops | bytes accessed | tf_op | source)
XLA Modules:
  0.0 290.8 jit_solution(15483379342645158404)
XLA Ops:
  8.8 2.2 copy.33
  11.1 2.3 copy.40
  13.3 15.7 %gather_fusion = bf16[4096,16]{1,0:T(8,128)(2,1)} fusion(bf16[16,4096]{0,1:T(8,128)(2,1)} %copy.33, s32[4096]{0:T(1024)S(1)} %fusion.23), kind=kCustom, calls=%fused_computation.clone | custom fusion | bytes 278528 | tf_op jit(solution)/shard_map/jit(_take)/gather | solution.py:31
  29.0 15.6 %gather_fusion.2 = bf16[4096,16]{1,0:T(8,128)(2,1)} fusion(bf16[16,4096]{0,1:T(8,128)(2,1)} %copy.40, s32[4096]{0:T(1024)S(1)} %fusion.23), kind=kCustom, calls=%fused_computation.2.clone | custom fusion | bytes 278528 | tf_op jit(solution)/shard_map/jit(_take)/gather | solution.py:32
  44.6 3.6 %broadcast_select_fusion = (bf16[4096,16]{1,0:T(8,128)(2,1)S(1)}, bf16[4096,16]{1,0:T(8,128)(2,1)S(1)}) fusion(bf16[4096,16]{1,0:T(8,128)(2,1)} %gather_fusion.2, pred[4096]{0:T(1024)(128)(4,1)S(1)} %compare_and_fusion, bf16[4096,16]{1,0:T(8,128)(2,1)} %gather_fusion), kind=kLoop, calls=%fused_computation.29 | loop fusion | flops 131072 | bytes 528384 | tf_op jit(solution)/shard_map/jit(_take)/select_n | solution.py:32
  51.9 48.1 %all-reduce.3.cloned.1.call-done = (f32[6,16,128]{2,1,0:T(8,128)}, f32[6,16,128]{2,1,0:T(8,128)}) async-done(((f32[6,16,128]{2,1,0:T(8,128)}, f32[6,16,128]{2,1,0:T(8,128)}), (f32[6,16,128]{2,1,0:T(8,128)}, f32[6,16,128]{2,1,0:T(8,128)})) %all-reduce.3.cloned.1.call-update) | async-done | bytes 98320 | tf_op jit(solution)/shard_map/psum | solution.py:45
  100.8 1.5 gather_fusion.3
  102.4 4.4 %convolution_convert_fusion = bf16[128,16,128]{2,1,0:T(8,128)(2,1)} fusion(bf16[128,128,128]{2,1,0:T(8,128)(2,1)} %param.25, bf16[128,16,128]{2,1,0:T(8,128)(2,1)} %gather_fusion.3, pred[128]{0:T(512)(128)(4,1)S(1)} %compare_and_fusion.1), kind=kOutput, calls=%fused_computation.10 | convolution fusion | flops 67633152 | bytes 5243008 | tf_op jit(solution)/shard_map/qmi,qik->qmk/dot_general | solution.py:68
  106.8 13.0 %all-to-all-start.1 = ((bf16[128,16,128]{2,1,0:T(8,128)(2,1)}), bf16[128,16,128]{2,1,0:T(8,128)(2,1)}, u32[]{:S(2)}, u32[]{:S(2)}) async-start(bf16[128,16,128]{2,1,0:T(8,128)(2,1)} %convolution_convert_fusion), calls=%async_computation.1 | async-start | bytes 1048576 | tf_op jit(solution)/shard_map/all_to_all | solution.py:71
  119.9 1.5 gather_fusion.1
  121.4 2.0 broadcast_select_fusion.2
  123.5 15.0 %all-to-all-done.1 = bf16[128,16,128]{2,1,0:T(8,128)(2,1)} async-done(((bf16[128,16,128]{2,1,0:T(8,128)(2,1)}), bf16[128,16,128]{2,1,0:T(8,128)(2,1)}, u32[]{:S(2)}, u32[]{:S(2)}) %all-to-all-start.1) | async-done | bytes 524320 | tf_op jit(solution)/shard_map/all_to_all | solution.py:71
  138.5 5.8 %all-to-all-start = ((bf16[128,16,128]{2,1,0:T(8,128)(2,1)}), bf16[128,16,128]{2,1,0:T(8,128)(2,1)}, u32[]{:S(2)}, u32[]{:S(2)}) async-start(bf16[128,16,128]{2,1,0:T(8,128)(2,1)} %broadcast_select_fusion.2), calls=%async_computation | async-start | bytes 1048576 | tf_op jit(solution)/shard_map/all_to_all | solution.py:67
  145.5 16.4 %all-to-all-done = bf16[128,16,128]{2,1,0:T(8,128)(2,1)} async-done(((bf16[128,16,128]{2,1,0:T(8,128)(2,1)}), bf16[128,16,128]{2,1,0:T(8,128)(2,1)}, u32[]{:S(2)}, u32[]{:S(2)}) %all-to-all-start) | async-done | bytes 524320 | tf_op jit(solution)/shard_map/all_to_all | solution.py:67
  161.9 4.7 %fusion.36 = f32[128,16,128]{2,1,0:T(8,128)S(1)} fusion(bf16[128,16,128]{2,1,0:T(8,128)(2,1)} %all-to-all-done, bf16[128,128,128]{2,1,0:T(8,128)(2,1)} %param.25), kind=kOutput, calls=%fused_computation.65 | convolution fusion | flops 67108864 | bytes 5767168 | tf_op jit(solution)/shard_map/qmk,qik->qmi/dot_general | solution.py:72
  166.5 1.4 fusion.12
  167.9 17.3 %all-gather.5.cloned.1.call-done = f32[384,16,128]{2,1,0:T(8,128)} async-done(((f32[6,16,128]{2,1,0:T(8,128)}), f32[384,16,128]{2,1,0:T(8,128)}) %all-gather.5.cloned.1.call-update) | async-done | bytes 3145744 | tf_op jit(solution)/shard_map/all_gather | solution.py:49
  185.2 4.7 %fusion = f32[6,1,16,128]{3,1,2,0:T(1,128)S(1)} fusion(f32[64,6,16,128]{3,2,1,0:T(8,128)} %bitcast.100, pred[6,64,1,1]{1,0,2,3:T(8,128)(4,1)S(1)} %fusion.32), kind=kOutput, calls=%fused_computation.6 | convolution fusion | flops 9437184 | bytes 3195264 | tf_op jit(solution)/shard_map/lr,rlmk->lmk/dot_general | solution.py:60
  192.7 12.2 %scatter_custom_fusion.1 = bf16[16,4096]{0,1:T(8,128)(2,1)} fusion(s32[4096]{0:T(1024)S(1)} %bitcast.107, bf16[4096,16]{1,0:T(8,128)(2,1)} %copy.46, bf16[]{:T(256)} %constant.22.clone.1), kind=kCustom, calls=%fused_computation.34 | custom fusion | bytes 131584 | tf_op jit(solution)/shard_map/scatter | solution.py:100
  205.0 2.2 copy.48
  207.1 57.0 %all-gather.3.cloned.1.call-done = f32[384,16,128]{2,1,0:T(8,128)} async-done(((f32[6,16,128]{2,1,0:T(8,128)}), f32[384,16,128]{2,1,0:T(8,128)}) %all-gather.3.cloned.1.call-update) | async-done | bytes 3145744 | tf_op jit(solution)/shard_map/all_gather | solution.py:48
  264.2 4.7 %fusion.2 = f32[6,1,16,128]{3,1,2,0:T(1,128)S(1)} fusion(f32[64,6,16,128]{3,2,1,0:T(8,128)} %bitcast.99, pred[6,64,1,1]{1,0,2,3:T(8,128)(4,1)S(1)} %fusion.32), kind=kOutput, calls=%fused_computation.8 | convolution fusion | flops 9437184 | bytes 3195264 | tf_op jit(solution)/shard_map/lr,rlmk->lmk/dot_general | solution.py:59
  270.5 1.3 copy.39
  271.9 11.4 %scatter_custom_fusion = bf16[16,4096]{0,1:T(8,128)(2,1)S(1)} fusion(s32[4096]{0:T(1024)S(1)} %bitcast.108, bf16[4096,16]{1,0:T(8,128)(2,1)} %copy.39, bf16[]{:T(256)} %constant.22.clone.1), kind=kCustom, calls=%fused_computation.36 | custom fusion | bytes 131584 | tf_op jit(solution)/shard_map/scatter | solution.py:99
  (68 shorter events, 12.7 us)
Async XLA Ops:
  7.2 183.8 %copy-start = (bf16[16,256,256]{2,1,0:T(8,128)(2,1)S(1)}, bf16[16,256,256]{2,1,0:T(8,128)(2,1)}, u32[]{:S(2)}) copy-start(bf16[16,256,256]{2,1,0:T(8,128)(2,1)} %param.19) | copy-start | bytes 6291460
  7.2 92.8 %all-reduce.3.cloned.1.call-start = ((), (), s32[]{:S(2)}) async-start(), calls=%async_computation.4 | async-start | bytes 196608 | tf_op jit(solution)/shard_map/psum | solution.py:45
  13.3 34.9 %copy-start.1 = (bf16[16,128,256]{2,1,0:T(8,128)(2,1)S(1)}, bf16[16,128,256]{2,1,0:T(8,128)(2,1)}, u32[]{:S(2)}) copy-start(bf16[16,128,256]{2,1,0:T(8,128)(2,1)} %param.18) | copy-start | bytes 3145732
  48.2 1.0 copy-start.2
  48.2 1.4 copy-start.4
  48.2 1.4 copy-start.6
  48.2 1.9 copy-start.10
  48.2 2.7 copy-start.9
  48.2 52.5 %copy-start.14 = (s32[1,128]{1,0:T(1,128)S(1)}, s32[1,128]{1,0:T(1,128)}, u32[]{:S(2)}) copy-start(s32[1,128]{1,0:T(1,128)} %param.24) | copy-start | bytes 1540
  51.8 133.4 %all-gather.5.cloned.1.call-start = ((), (), s32[]{:S(2)}) async-start(), calls=%async_computation.3 | async-start | bytes 3194880 | tf_op jit(solution)/shard_map/all_gather | solution.py:49
  100.0 164.2 %all-gather.3.cloned.1.call-start = ((), (), s32[]{:S(2)}) async-start(), calls=%async_computation.2 | async-start | bytes 3194880 | tf_op jit(solution)/shard_map/all_gather | solution.py:48
  102.4 17.5 %copy-start.15 = (s32[1,128]{1,0:T(1,128)S(1)}, s32[1,128]{1,0:T(1,128)}, u32[]{:S(2)}) copy-start(s32[1,128]{1,0:T(1,128)} %param.23) | copy-start | bytes 1540
  106.8 37.4 %copy-start.13 = (s32[1,4096]{1,0:T(1,128)S(1)}, s32[1,4096]{1,0:T(1,128)}, u32[]{:S(2)}) copy-start(s32[1,4096]{1,0:T(1,128)} %param.17) | copy-start | bytes 49156
  106.8 31.7 %all-to-all-start.1 = ((bf16[128,16,128]{2,1,0:T(8,128)(2,1)}), bf16[128,16,128]{2,1,0:T(8,128)(2,1)}, u32[]{:S(2)}, u32[]{:S(2)}) async-start(bf16[128,16,128]{2,1,0:T(8,128)(2,1)} %convolution_convert_fusion), calls=%async_computation.1 | async-start | bytes 1048576 | tf_op jit(solution)/shard_map/all_to_all | solution.py:71
  138.5 23.4 %all-to-all-start = ((bf16[128,16,128]{2,1,0:T(8,128)(2,1)}), bf16[128,16,128]{2,1,0:T(8,128)(2,1)}, u32[]{:S(2)}, u32[]{:S(2)}) async-start(bf16[128,16,128]{2,1,0:T(8,128)(2,1)} %broadcast_select_fusion.2), calls=%async_computation | async-start | bytes 1048576 | tf_op jit(solution)/shard_map/all_to_all | solution.py:67
  185.2 4.9 %copy-start.7 = (bf16[16,128,128]{2,1,0:T(8,128)(2,1)S(1)}, bf16[16,128,128]{2,1,0:T(8,128)(2,1)}, u32[]{:S(2)}) copy-start(bf16[16,128,128]{2,1,0:T(8,128)(2,1)} %param.20) | copy-start | bytes 1572868
  185.2 5.7 %copy-start.5 = (bf16[4096,16]{1,0:T(8,128)(2,1)S(1)}, bf16[4096,16]{1,0:T(8,128)(2,1)}, u32[]{:S(2)}) copy-start(bf16[4096,16]{1,0:T(8,128)(2,1)} %copy-done.4) | copy-start | bytes 393220
  191.4 77.5 %copy-start.11 = (bf16[6,128,128]{2,1,0:T(8,128)(2,1)S(1)}, bf16[6,128,128]{2,1,0:T(8,128)(2,1)}, u32[]{:S(2)}) copy-start(bf16[6,128,128]{2,1,0:T(8,128)(2,1)} %param.22) | copy-start | bytes 589828
  192.7 76.4 %copy-start.12 = (f32[16,16,128]{2,0,1:T(8,128)S(1)}, f32[16,16,128]{2,0,1:T(8,128)}, u32[]{:S(2)}) copy-start(f32[16,16,128]{2,0,1:T(8,128)} %fusion.12) | copy-start | bytes 393220
  264.2 5.0 %copy-start.8 = (bf16[16,128,128]{2,1,0:T(8,128)(2,1)S(1)}, bf16[16,128,128]{2,1,0:T(8,128)(2,1)}, u32[]{:S(2)}) copy-start(bf16[16,128,128]{2,1,0:T(8,128)(2,1)} %param.20) | copy-start | bytes 1572868
  264.2 5.6 %copy-start.3 = (bf16[4096,16]{1,0:T(8,128)(2,1)S(1)}, bf16[4096,16]{1,0:T(8,128)(2,1)}, u32[]{:S(2)}) copy-start(bf16[4096,16]{1,0:T(8,128)(2,1)} %copy-done.2) | copy-start | bytes 393220
Sparse Core Ops, SparseCore 0:
  52.0 48.0 all-reduce.2
  103.1 82.0 all-gather.4
  188.4 75.7 all-gather.2
where the time goes:
time: 292 us; the launch traced here: 291 us
  waiting for transfers between devices  154 us (53%)
  local copies, waits for them, and re-layouts  68.9 us (24%)
  matrix products  27.2 us (9%)
  starting transfers between devices  18.9 us (6%)
  between operations  14 us (5%)
  other arithmetic  7.35 us (3%)
    all_gather x1, waiting for transfers between devices, shards(): lax.all_gather(fwd_terms, 'sub', axis=0, tiled=True)  57 us
    psum x1, waiting for transfers between devices, shards(): fwd_terms, bwd_terms = lax.psum((fwd_terms, bwd_terms), 'blk')  48.1 us
    all_gather x1, waiting for transfers between devices, shards(): lax.all_gather(bwd_terms, 'sub', axis=0, tiled=True)  17.3 us
    all_to_all x1, waiting for transfers between devices, shards(): lax.all_to_all(outgoing, 'sub', split_axis=0, concat_axis=0, tiled=True)  16.4 us
    gather x1, local copies, waits for them, and re-layouts, shards(): jnp.take(inputs, ordering, axis=1).reshape(rhs_count, leaf_count, leaf_size)  15.7 us
    gather x1, local copies, waits for them, and re-layouts, shards(): jnp.take(adjoint_in, ordering, axis=1)  15.6 us
    all_to_all x1, waiting for transfers between devices, shards(): lax.all_to_all(returned_src, 'sub', split_axis=0, concat_axis=0, tiled=True)  15 us
    all_to_all x1, starting transfers between devices, shards(): lax.all_to_all(returned_src, 'sub', split_axis=0, concat_axis=0, tiled=True)  13 us
  transfers between devices with their start and end apart: 5, of which 5 were waited for; matrix products, arithmetic and copies ran while one was open for 13% of the time, Pallas kernels for 0%

commit v1 on v0

v1 whole, which is shorter than its diff:
```python
import jax
import jax.numpy as jnp
from jax import lax
from jax.experimental import pallas as pl
from jax.experimental.pallas import tpu as pltpu
from jax.sharding import PartitionSpec as P

F32 = jnp.float32
BF16 = jnp.bfloat16
MESH = pl.DeviceIdType.MESH

FWD = (0, 1, -1, 2, -2, 3, -3, 4)
BWD = (4, 3, -3, 2, -2, 1, -1, 0)
FPOS = {d: i for i, d in enumerate(FWD)}
BPOS = {d: i for i, d in enumerate(BWD)}
FBATCH = ((0, 3), (3, 5), (5, 7), (7, 8))
BBATCH = ((0, 1), (1, 3), (3, 5), (5, 8))


def nt(a, b):
    return lax.dot_general(a, b, (((1,), (1,)), ((), ())), preferred_element_type=F32)


def nn(a, b):
    return lax.dot_general(a, b, (((1,), (0,)), ((), ())), preferred_element_type=F32)


def batch_nt(a, b):
    return lax.dot_general(a, b, (((2,), (2,)), ((0,), (0,))), preferred_element_type=F32)


def batch_nn(a, b):
    return lax.dot_general(a, b, (((2,), (1,)), ((0,), (0,))), preferred_element_type=F32)


def split(a):
    high = a.astype(BF16)
    low = (a - high.astype(F32)).astype(BF16)
    return high, low


def stacked(a):
    high, low = split(a)
    return jnp.concatenate([high, low], axis=0)


def folded(a):
    half = a.shape[0] // 2
    return a[:half] + a[half:]


def xor3(a, e):
    total = 0
    for bit in range(3):
        value = lax.rem(a // (1 << bit), 2)
        if (e >> bit) & 1:
            value = 1 - value
        total = total + value * (1 << bit)
    return total


def level_of(e):
    return 0 if e == 1 else (1 if e < 4 else 2)


def kernel(
    inp, adj, pmap, slist, tlist,
    bases_h, near_h, trans_h, up_h, down_h, coup_h,
    out_x, out_a,
    bases, near, trans, up, down, coup,
    xl, oh, gath, nterm, diff_n, diff_t, acc,
    ag, ws, lists, fsend, frecv, bsend, brecv,
    cws, cwr, ccs, ccr,
    lxs, lxr, lws, lwr, lzs, lzr, lar,
    local_sem, ag_s, ag_r, list_s, list_r, f_s, f_r, b_s, b_r,
    cw_s, cw_r, cc_s, cc_r, lx_s, lx_r, lw_s, lw_r, lz_s, lz_r, la_s, la_r,
):
    s = lax.axis_index("sub")
    b = lax.axis_index("blk")
    z = s // 8
    w = lax.rem(s, 8)

    loads = []
    for i, (src, dst) in enumerate(
        ((bases_h, bases), (trans_h, trans), (up_h, up), (down_h, down), (coup_h, coup), (near_h, near))
    ):
        copy = pltpu.make_async_copy(src, dst, local_sem.at[i])
        copy.start()
        loads.append(copy)

    def z_dev(d):
        return (lax.rem(z + d + 8, 8) * 8 + w, b)

    def zx_dev(e):
        return (xor3(z, e) * 8 + w, b)

    def w_dev(e):
        return (z * 8 + xor3(w, e), b)

    def x_dev(d):
        return (s, lax.rem(b + d, 4))

    barrier = pltpu.get_barrier_semaphore()
    for e in range(1, 8):
        pl.semaphore_signal(barrier, inc=1, device_id=zx_dev(e), device_id_type=MESH)
        pl.semaphore_signal(barrier, inc=1, device_id=w_dev(e), device_id_type=MESH)
    for d in range(1, 4):
        pl.semaphore_signal(barrier, inc=1, device_id=x_dev(d), device_id_type=MESH)

    def send(src, dst, ssem, rsem, dev):
        copy = pltpu.make_async_remote_copy(
            src_ref=src, dst_ref=dst, send_sem=ssem, recv_sem=rsem, device_id=dev, device_id_type=MESH
        )
        copy.start()
        return copy

    sent = []

    row = lax.broadcasted_iota(jnp.int32, (256, 256), 0)
    col = lax.broadcasted_iota(jnp.int32, (256, 256), 1)
    diff_n[...] = (row - (col & 15)).astype(F32)
    diff_t[...] = (col - (row & 15)).astype(F32)
    for h in range(16):
        xl[h * 32 : h * 32 + 16, :] = inp[:, h * 256 : (h + 1) * 256]
        xl[h * 32 + 16 : h * 32 + 32, :] = adj[:, h * 256 : (h + 1) * 256]
    lists[0] = jnp.broadcast_to(slist[...].astype(F32), (16, 128)).astype(BF16)
    targets = jnp.broadcast_to(tlist[...].astype(F32), (16, 128))

    loads[0].wait()
    loads[1].wait()

    def leaf_in(leaf, carry):
        xd, wd = carry
        off = pl.multiple_of(leaf * 256, 256)
        places = pmap[:, pl.ds(off, 256)]
        low, high = places & 255, places >> 8
        hot = jnp.where(lax.broadcasted_iota(jnp.int32, (256, 256), 0) == low, 1.0, 0.0).astype(BF16)
        oh[:, pl.ds(off, 256)] = hot
        every = nn(xl[...], hot)
        vals = jnp.zeros((32, 256), F32)
        for h in range(16):
            vals = vals + jnp.where(high == h, every[h * 32 : (h + 1) * 32, :], 0.0)
        vals = vals.astype(BF16)
        gath[leaf] = vals
        skel = nt(vals, bases[leaf]).astype(BF16)
        rows = pl.ds(pl.multiple_of(leaf * 16, 16), 16)
        ag[0, rows, :] = skel[:16]
        ws[rows, :] = skel[16:]
        return xd + nt(skel[:16], trans[leaf]), wd + nn(skel[16:], trans[leaf])

    zero = jnp.zeros((16, 128), F32)
    xd, wd = lax.fori_loop(0, 16, leaf_in, (zero, zero))

    pl.semaphore_wait(barrier, 17)
    list_in = {}
    for i, d in enumerate((1, -1, 2, -2, 3, -3, 4)):
        origin = 4 if d == 4 else -d
        list_in[origin] = send(lists.at[0], lists.at[FPOS[origin]], list_s.at[i], list_r.at[i], z_dev(d))
    cw_in, cc_in = [], []

    def ag_cw(k):
        dst = 4 if k == 3 else -(k + 1)
        cw_in.append(send(ag.at[FPOS[-k]], ag.at[FPOS[dst]], ag_s.at[k], ag_r.at[k], z_dev(1)))

    def ag_cc(k):
        cc_in.append(send(ag.at[FPOS[k]], ag.at[FPOS[k + 1]], ag_s.at[4 + k], ag_r.at[4 + k], z_dev(-1)))

    ag_cw(0)
    ag_cc(0)

    loads[2].wait()
    loads[3].wait()
    xd2, wd2 = stacked(xd), stacked(wd)
    for v in range(6):
        cx = folded(nt(xd2, up[v]))
        cw = folded(nn(wd2, down[v]))
        lxs[0, v] = cx[:8]
        lxs[1, v] = cx[8:]
        lxs[2, v] = cw[:8]
        lxs[3, v] = cw[8:]
    lx_in = [
        send(lxs.at[lax.rem(b + d, 4)], lxr.at[d - 1], lx_s.at[d - 1], lx_r.at[d - 1], x_dev(d)) for d in range(1, 4)
    ]

    lane = lax.broadcasted_iota(jnp.int32, (16, 128), 1)
    spread = (
        (lax.broadcasted_iota(jnp.int32, (128, 256), 0) & 15) == (lax.broadcasted_iota(jnp.int32, (128, 256), 1) >> 4)
    ).astype(F32).astype(BF16)
    spread_t = (
        (lax.broadcasted_iota(jnp.int32, (256, 128), 1) & 15) == (lax.broadcasted_iota(jnp.int32, (256, 128), 0) >> 4)
    ).astype(F32)
    ones = jnp.ones((128, 256), BF16)

    def chosen(values, chunk):
        return jnp.where((lane >> 4) == chunk, values * 16.0, 0.0)

    def sum_matrix(values, chunk):
        line = nn(chosen(values, chunk).astype(BF16), spread)[:1]
        return jnp.where(diff_n[...] == line, 1.0, 0.0).astype(BF16)

    def pick_matrix(values, chunk):
        part = (spread_t * chosen(values, chunk)[:1]).astype(BF16)
        return jnp.where(diff_t[...] == nn(part, ones), 1.0, 0.0).astype(BF16)

    loads[4].wait()
    f_in, b_in = [], []

    def plane_send(buf_s, buf_r, lo, hi, sems_s, sems_r, k):
        copies = []
        for e in range(1, 8):
            copies.append(
                send(
                    buf_s.at[xor3(w, e), pl.ds(lo, hi - lo)],
                    buf_r.at[w, pl.ds(lo, hi - lo)],
                    sems_s.at[k, e - 1],
                    sems_r.at[k, e - 1],
                    w_dev(e),
                )
            )
        buf_r[w, lo:hi] = buf_s[w, lo:hi]
        return copies

    def ret_chunk(pos):
        chunk = lax.rem(z + BWD[pos] + 8, 8)
        picked = nn(pick_matrix(targets, chunk), ws[...]).astype(BF16).reshape(16, 16, 128)
        mats = coup[pl.ds(pl.multiple_of(chunk * 16, 16), 16)]
        ret = batch_nn(picked, mats).astype(BF16)
        bsend[:, pos] = ret.reshape(8, 32, 128)

    for k, (lo, hi) in enumerate(BBATCH):
        for pos in range(lo, hi):
            ret_chunk(pos)
        b_in.append(plane_send(bsend, brecv, lo, hi, b_s, b_r, k))

    def select(delta):
        pos = FPOS[delta]
        if delta:
            list_in[delta].wait_recv()
        picked = nn(pick_matrix(lists[pos].astype(F32), z), ag[pos]).astype(BF16)
        fsend[:, pos] = picked.reshape(8, 32, 128)

    def f_batch(k):
        lo, hi = FBATCH[k]
        for pos in range(lo, hi):
            select(FWD[pos])
        f_in.append(plane_send(fsend, frecv, lo, hi, f_s, f_r, k))

    def part(delta):
        values = lists[FPOS[delta]].astype(F32)
        return nn(sum_matrix(values, z), brecv[:, BPOS[delta]].reshape(256, 128))

    def wait_all(copies):
        for copy in copies:
            copy.wait_recv()

    rs_cw, rs_cc = [], []

    def rs_cw_send(k, value):
        cws[k] = value.astype(BF16)
        rs_cw.append(send(cws.at[k], cwr.at[k], cw_s.at[k], cw_r.at[k], z_dev(1)))

    def rs_cc_send(k, value):
        ccs[k] = value.astype(BF16)
        rs_cc.append(send(ccs.at[k], ccr.at[k], cc_s.at[k], cc_r.at[k], z_dev(-1)))

    def near_part(lo, hi):
        def body(leaf, carry):
            nterm[leaf, 0:16, :] = nt(gath[leaf, 0:16, :], near[leaf])
            nterm[leaf, 16:32, :] = nn(gath[leaf, 16:32, :], near[leaf])
            return carry

        lax.fori_loop(lo, hi, body, 0)

    def list_chunk(pos, total):
        chunk = lax.rem(z + FWD[pos] + 8, 8)
        inc = frecv[:, pos].reshape(16, 16, 128)
        mats = coup[pl.ds(pl.multiple_of(chunk * 16, 16), 16)]
        terms = batch_nt(inc, mats).reshape(256, 128)
        high, low = split(terms)
        both = nn(sum_matrix(targets, chunk), jnp.concatenate([high, low], axis=1))
        return total + both[:, :128] + both[:, 128:]

    cw_in[0].wait_recv()
    ag_cw(1)
    cc_in[0].wait_recv()
    ag_cc(1)
    f_batch(0)

    wait_all(lx_in)
    mine = lxs[b] + lxr[0] + lxr[1] + lxr[2]
    for v in range(3):
        lws[v, 0] = mine[v]
        lws[v, 1:4] = mine[3:6]
    lw_in = [
        send(lws.at[level_of(e)], lwr.at[e - 1], lw_s.at[e - 1], lw_r.at[e - 1], w_dev(e)) for e in range(1, 8)
    ]

    wait_all(b_in[0])
    list_in[4].wait_recv()
    rs_cc_send(0, part(4))
    wait_all(b_in[1])
    list_in[3].wait_recv()
    list_in[-3].wait_recv()
    rs_cw_send(0, part(3))
    loads[5].wait()
    near_part(0, 4)
    here = part(-3)
    rs_cc[0].wait_recv()
    rs_cc_send(1, here + ccr[0].astype(F32))

    cw_in[1].wait_recv()
    ag_cw(2)
    cc_in[1].wait_recv()
    ag_cc(2)
    list_in[2].wait_recv()
    list_in[-2].wait_recv()

    def f_batch_listed(k):
        lo, hi = FBATCH[k]
        for pos in range(lo, hi):
            picked = nn(pick_matrix(lists[pos].astype(F32), z), ag[pos]).astype(BF16)
            fsend[:, pos] = picked.reshape(8, 32, 128)
        f_in.append(plane_send(fsend, frecv, lo, hi, f_s, f_r, k))

    f_batch_listed(1)

    wait_all(lw_in)
    upper = mine[3:6]
    for e in range(1, 8):
        upper = upper + lwr[e - 1, 1:4]
    for v in range(3):
        lzs[v] = upper[v]
    lz_in = [send(lzs.at[level_of(e)], lzr.at[e - 1], lz_s.at[e - 1], lz_r.at[e - 1], zx_dev(e)) for e in range(1, 8)]

    wait_all(b_in[2])
    here_p, here_m = part(2), part(-2)
    rs_cw[0].wait_recv()
    rs_cw_send(1, here_p + cwr[0].astype(F32))
    rs_cc[1].wait_recv()
    rs_cc_send(2, here_m + ccr[1].astype(F32))
    near_part(4, 8)

    cw_in[2].wait_recv()
    ag_cw(3)
    cc_in[2].wait_recv()
    f_batch_listed(2)

    wait_all(lz_in)
    quarter = [
        lwr[0, 0],
        lwr[1, 0] + lwr[2, 0],
        lwr[3, 0] + lwr[4, 0] + lwr[5, 0] + lwr[6, 0],
        lzr[0],
        lzr[1] + lzr[2],
        lzr[3] + lzr[4] + lzr[5] + lzr[6],
    ]
    for v in range(6):
        lar[b, v] = quarter[v]
    la_in = [send(lar.at[b], lar.at[b], la_s.at[d - 1], la_r.at[d - 1], x_dev(d)) for d in range(1, 4)]

    wait_all(b_in[3])
    here_p, here_m, own = part(1), part(-1), part(0)
    rs_cw[1].wait_recv()
    rs_cw_send(2, here_p + cwr[1].astype(F32))
    rs_cc[2].wait_recv()
    rs_cc_send(3, here_m + ccr[2].astype(F32))

    near_part(8, 16)
    wait_all(f_in[0])
    lx = jnp.zeros((256, 128), F32)
    for pos in range(0, 3):
        lx = list_chunk(pos, lx)

    cw_in[3].wait_recv()
    f_batch_listed(3)

    for k in (1, 2):
        wait_all(f_in[k])
        for pos in range(*FBATCH[k]):
            lx = list_chunk(pos, lx)

    wait_all(la_in)
    yd = jnp.zeros((32, 128), F32)
    zd = jnp.zeros((32, 128), F32)
    for v in range(6):
        sx = jnp.concatenate([lar[0, v], lar[1, v]], axis=0)
        sw = jnp.concatenate([lar[2, v], lar[3, v]], axis=0)
        yd = yd + nt(stacked(sx), down[v])
        zd = zd + nn(stacked(sw), up[v])
    yd2, zd2 = stacked(folded(yd)), stacked(folded(zd))

    rs_cw[2].wait_recv()
    rs_cc[3].wait_recv()
    lw = own + cwr[2].astype(F32) + ccr[3].astype(F32)

    wait_all(f_in[3])
    lx = list_chunk(7, lx)

    acc[...] = jnp.zeros_like(acc)
    lsum = jnp.concatenate([lx.reshape(16, 16, 128), lw.reshape(16, 16, 128)], axis=1)


    for leaf in range(16):
        off = leaf * 256
        ys = folded(nn(yd2, trans[leaf]))
        zs = folded(nt(zd2, trans[leaf]))
        exp = (jnp.concatenate([ys, zs], axis=0) + lsum[leaf]).astype(BF16)
        vals = nn(exp, bases[leaf]) + nterm[leaf]
        high = pmap[:, off : off + 256] >> 8
        vals = vals.astype(BF16).astype(F32)
        masked = jnp.concatenate([jnp.where(high == h, vals, 0.0) for h in range(16)], axis=0).astype(BF16)
        acc[...] += nt(masked, oh[:, off : off + 256])

    for h in range(16):
        out_x[:, h * 256 : (h + 1) * 256] = acc[h * 32 : h * 32 + 16, :].astype(BF16)
        out_a[:, h * 256 : (h + 1) * 256] = acc[h * 32 + 16 : h * 32 + 32, :].astype(BF16)

    for copies in [list(list_in.values()), cw_in, cc_in, lx_in, lw_in, lz_in, la_in, rs_cw, rs_cc] + f_in + b_in:
        for copy in copies:
            copy.wait_send()


def shards(inputs, adjoint_in, panel_map, bases, near, trans, up, down, send_list, target_leaf, coup):
    vmem = pl.BlockSpec(memory_space=pltpu.VMEM)
    hbm = pl.BlockSpec(memory_space=pl.ANY)
    dma = pltpu.SemaphoreType.DMA
    return pl.pallas_call(
        kernel,
        out_shape=(jax.ShapeDtypeStruct((16, 4096), BF16), jax.ShapeDtypeStruct((16, 4096), BF16)),
        in_specs=[vmem] * 5 + [hbm] * 6,
        out_specs=(vmem, vmem),
        scratch_shapes=[
            pltpu.VMEM((16, 128, 256), BF16),
            pltpu.VMEM((16, 256, 256), BF16),
            pltpu.VMEM((16, 128, 128), BF16),
            pltpu.VMEM((6, 128, 128), BF16),
            pltpu.VMEM((6, 128, 128), BF16),
            pltpu.VMEM((128, 128, 128), BF16),
            pltpu.VMEM((512, 256), BF16),
            pltpu.VMEM((256, 4096), BF16),
            pltpu.VMEM((16, 32, 256), BF16),
            pltpu.VMEM((16, 32, 256), F32),
            pltpu.VMEM((256, 256), F32),
            pltpu.VMEM((256, 256), F32),
            pltpu.VMEM((512, 256), F32),
            pltpu.VMEM((8, 256, 128), BF16),
            pltpu.VMEM((256, 128), BF16),
            pltpu.VMEM((8, 16, 128), BF16),
            pltpu.VMEM((8, 8, 32, 128), BF16),
            pltpu.VMEM((8, 8, 32, 128), BF16),
            pltpu.VMEM((8, 8, 32, 128), BF16),
            pltpu.VMEM((8, 8, 32, 128), BF16),
            pltpu.VMEM((3, 256, 128), BF16),
            pltpu.VMEM((3, 256, 128), BF16),
            pltpu.VMEM((4, 256, 128), BF16),
            pltpu.VMEM((4, 256, 128), BF16),
            pltpu.VMEM((4, 6, 8, 128), F32),
            pltpu.VMEM((3, 6, 8, 128), F32),
            pltpu.VMEM((3, 4, 8, 128), F32),
            pltpu.VMEM((7, 4, 8, 128), F32),
            pltpu.VMEM((3, 8, 128), F32),
            pltpu.VMEM((7, 8, 128), F32),
            pltpu.VMEM((4, 6, 8, 128), F32),
            dma((6,)),
            dma((7,)), dma((7,)),
            dma((7,)), dma((7,)),
            dma((4, 7)), dma((4, 7)),
            dma((4, 7)), dma((4, 7)),
            dma((3,)), dma((3,)),
            dma((4,)), dma((4,)),
            dma((3,)), dma((3,)),
            dma((7,)), dma((7,)),
            dma((7,)), dma((7,)),
            dma((3,)), dma((3,)),
        ],
        compiler_params=pltpu.CompilerParams(
            collective_id=0, has_side_effects=True, vmem_limit_bytes=48 * 1024 * 1024
        ),
    )(inputs, adjoint_in, panel_map, send_list, target_leaf, bases, near, trans, up, down, coup)


def solution(mesh):
    each = ("sub", "blk")
    return jax.shard_map(
        shards,
        mesh=mesh,
        in_specs=(
            P(None, each),
            P(None, each),
            P(each, None),
            P(each, None, None),
            P(each, None, None),
            P(each, None, None),
            P(each, None, None),
            P(each, None, None),
            P(each, None),
            P(each, None),
            P(each, None, None),
        ),
        out_specs=(P(None, each), P(None, each)),
        check_vma=False,
    )
```

time: 292 us -> 58.9 us (0.20)
  waiting for transfers between devices: 154 us -> 0 us
  local copies, waits for them, and re-layouts: 68.9 us -> 10.8 us
  Pallas kernels: 0 us -> 47 us
  matrix products: 27.2 us -> 0 us
  starting transfers between devices: 18.9 us -> 0 us
  between operations: 14 us -> 0.66 us
  other arithmetic: 7.35 us -> 0 us
    all_gather x2 -> x0, waiting for transfers between devices: 74.3 us -> none  [the longest x1 57 us: shards(): lax.all_gather(fwd_terms, 'sub', axis=0, tiled=True)]
    psum x1 -> x0, waiting for transfers between devices: 48.1 us -> none  [shards(): fwd_terms, bwd_terms = lax.psum((fwd_terms, bwd_terms), 'blk')]
    pallas_call x0 -> x1, Pallas kernels: none -> 47 us  [shards(): pl.pallas_call(kernel, out_shape=(jax.ShapeDtypeStruct((16, 4096), BF16),...]
    gather x4 -> x0, local copies, waits for them, and re-layouts: 34.3 us -> none  [the longest x1 15.7 us: shards(): jnp.take(inputs, ordering, axis=1).reshape(rhs_count, leaf_count, leaf_size)]
    all_to_all x2 -> x0, waiting for transfers between devices: 31.3 us -> none  [the longest x1 16.4 us: shards(): lax.all_to_all(outgoing, 'sub', split_axis=0, concat_axis=0, tiled=True)]
    dot_general x20 -> x0, matrix products: 27.2 us -> none  [the longest x1 4.73 us: shards(): sib_fwd = jnp.einsum('lr,rlmk->lmk', weights, all_fwd, precision=HIGHEST)]
    scatter x2 -> x0, local copies, waits for them, and re-layouts: 23.6 us -> none  [the longest x1 12.2 us: shards(): adjoint_product = jnp.zeros_like(adjoint_in).at[:, ordering].set(bwd_vals)]
    all_to_all x2 -> x0, starting transfers between devices: 18.8 us -> none  [the longest x1 13 us: shards(): lax.all_to_all(returned_src, 'sub', split_axis=0, concat_axis=0, tiled=True)]
  transfers between devices with their start and end apart: 5 -> 0, of which waited for: 5 -> 0; matrix products, arithmetic and copies ran while one was open for 13% -> 0% of each run, Pallas kernels for 0% -> 0%
where the time goes in v1:
time: 58.9 us; the launch traced here: 58.5 us
  Pallas kernels  47 us (80%)
  local copies, waits for them, and re-layouts  10.8 us (18%)
  between operations  0.66 us (1%)
    pallas_call x1, Pallas kernels, shards(): pl.pallas_call(kernel, out_shape=(jax.ShapeDtypeStruct((16, 4096), BF16),...  47 us
    unnamed x22, local copies, waits for them, and re-layouts  10.8 us

profile of v1, /device:TPU:1, one launch (start us, length us, event | category | flops | bytes accessed | tf_op | source)
XLA Modules:
  0.0 58.5 jit_solution(10128586672058600657)
XLA Ops:
  0.6 0.0 copy-start
  0.6 1.6 %copy-done = bf16[16,256,256]{2,1,0:T(8,128)(2,1)S(1)} copy-done((bf16[16,256,256]{2,1,0:T(8,128)(2,1)S(1)}, bf16[16,256,256]{2,1,0:T(8,128)(2,1)}, u32[]{:S(2)}) %copy-start) | copy-done | bytes 2097176
  2.2 0.0 copy-start.1
  2.2 1.2 %copy-done.1 = bf16[16,128,256]{2,1,0:T(8,128)(2,1)S(1)} copy-done((bf16[16,128,256]{2,1,0:T(8,128)(2,1)S(1)}, bf16[16,128,256]{2,1,0:T(8,128)(2,1)}, u32[]{:S(2)}) %copy-start.1) | copy-done | bytes 1048600
  3.5 0.0 copy-start.2
  3.5 1.0 %copy-done.2 = bf16[16,128,128]{2,1,0:T(8,128)(2,1)S(1)} copy-done((bf16[16,128,128]{2,1,0:T(8,128)(2,1)S(1)}, bf16[16,128,128]{2,1,0:T(8,128)(2,1)}, u32[]{:S(2)}) %copy-start.2) | copy-done | bytes 524312
  4.5 0.0 copy-start.3
  4.5 0.9 %copy-done.3 = bf16[6,128,128]{2,1,0:T(8,128)(2,1)S(1)} copy-done((bf16[6,128,128]{2,1,0:T(8,128)(2,1)S(1)}, bf16[6,128,128]{2,1,0:T(8,128)(2,1)}, u32[]{:S(2)}) %copy-start.3) | copy-done | bytes 196632
  5.4 0.0 copy-start.4
  5.4 0.9 %copy-done.4 = bf16[6,128,128]{2,1,0:T(8,128)(2,1)S(1)} copy-done((bf16[6,128,128]{2,1,0:T(8,128)(2,1)S(1)}, bf16[6,128,128]{2,1,0:T(8,128)(2,1)}, u32[]{:S(2)}) %copy-start.4) | copy-done | bytes 196632
  6.3 0.0 copy-start.5
  6.4 0.9 %copy-done.5 = bf16[16,4096]{1,0:T(8,128)(2,1)S(1)} copy-done((bf16[16,4096]{1,0:T(8,128)(2,1)S(1)}, bf16[16,4096]{1,0:T(8,128)(2,1)}, u32[]{:S(2)}) %copy-start.5) | copy-done | bytes 131096
  7.3 0.0 copy-start.6
  7.3 0.9 %copy-done.6 = bf16[16,4096]{1,0:T(8,128)(2,1)S(1)} copy-done((bf16[16,4096]{1,0:T(8,128)(2,1)S(1)}, bf16[16,4096]{1,0:T(8,128)(2,1)}, u32[]{:S(2)}) %copy-start.6) | copy-done | bytes 131096
  8.2 0.0 copy-start.7
  8.2 0.7 %copy-done.7 = s32[1,4096]{1,0:T(1,128)S(1)} copy-done((s32[1,4096]{1,0:T(1,128)S(1)}, s32[1,4096]{1,0:T(1,128)}, u32[]{:S(2)}) %copy-start.7) | copy-done | bytes 16408
  8.9 0.0 copy-start.8
  8.9 0.7 %copy-done.8 = s32[1,128]{1,0:T(1,128)S(1)} copy-done((s32[1,128]{1,0:T(1,128)S(1)}, s32[1,128]{1,0:T(1,128)}, u32[]{:S(2)}) %copy-start.8) | copy-done | bytes 536
  9.5 0.0 copy-start.9
  9.5 0.7 %copy-done.9 = s32[1,128]{1,0:T(1,128)S(1)} copy-done((s32[1,128]{1,0:T(1,128)S(1)}, s32[1,128]{1,0:T(1,128)}, u32[]{:S(2)}) %copy-start.9) | copy-done | bytes 536
  10.2 47.0 %shard_map.122 = (bf16[16,4096]{1,0:T(8,128)(2,1)S(1)}, bf16[16,4096]{1,0:T(8,128)(2,1)S(1)}) custom-call(bf16[16,4096]{1,0:T(8,128)(2,1)S(1)} %copy-done.5, bf16[16,4096]{1,0:T(8,128)(2,1)S(1)} %copy-done.6, s32[1,4096]{1,0:T(1,128)S(1)} %copy-done.7, s32[1,128]{1,0:T(1,128)S(1)} %copy-done.8, s32[1,128]{1,0:T(1,128)S(1)} %copy-done.9, ...), custom_call_target="tpu_custom_call" | custom-call | tf_op jit(solution)/shard_map/pallas_call | solution.py:427
  57.2 0.7 %copy.15 = bf16[16,4096]{1,0:T(8,128)(2,1)} copy(bf16[16,4096]{1,0:T(8,128)(2,1)S(1)} %get-tuple-element.4) | data formatting | bytes 262144
  57.8 0.7 %copy.16 = bf16[16,4096]{1,0:T(8,128)(2,1)} copy(bf16[16,4096]{1,0:T(8,128)(2,1)S(1)} %get-tuple-element.5) | data formatting | bytes 262144
Async XLA Ops:
  0.6 1.6 %copy-start = (bf16[16,256,256]{2,1,0:T(8,128)(2,1)S(1)}, bf16[16,256,256]{2,1,0:T(8,128)(2,1)}, u32[]{:S(2)}) copy-start(bf16[16,256,256]{2,1,0:T(8,128)(2,1)} %near_h.1) | copy-start | bytes 6291460
  2.2 1.2 %copy-start.1 = (bf16[16,128,256]{2,1,0:T(8,128)(2,1)S(1)}, bf16[16,128,256]{2,1,0:T(8,128)(2,1)}, u32[]{:S(2)}) copy-start(bf16[16,128,256]{2,1,0:T(8,128)(2,1)} %bases_h.1) | copy-start | bytes 3145732
  3.5 1.0 %copy-start.2 = (bf16[16,128,128]{2,1,0:T(8,128)(2,1)S(1)}, bf16[16,128,128]{2,1,0:T(8,128)(2,1)}, u32[]{:S(2)}) copy-start(bf16[16,128,128]{2,1,0:T(8,128)(2,1)} %trans_h.1) | copy-start | bytes 1572868
  4.5 0.9 %copy-start.3 = (bf16[6,128,128]{2,1,0:T(8,128)(2,1)S(1)}, bf16[6,128,128]{2,1,0:T(8,128)(2,1)}, u32[]{:S(2)}) copy-start(bf16[6,128,128]{2,1,0:T(8,128)(2,1)} %up_h.1) | copy-start | bytes 589828
  5.4 0.9 %copy-start.4 = (bf16[6,128,128]{2,1,0:T(8,128)(2,1)S(1)}, bf16[6,128,128]{2,1,0:T(8,128)(2,1)}, u32[]{:S(2)}) copy-start(bf16[6,128,128]{2,1,0:T(8,128)(2,1)} %down_h.1) | copy-start | bytes 589828
  6.3 0.9 %copy-start.5 = (bf16[16,4096]{1,0:T(8,128)(2,1)S(1)}, bf16[16,4096]{1,0:T(8,128)(2,1)}, u32[]{:S(2)}) copy-start(bf16[16,4096]{1,0:T(8,128)(2,1)} %inp.1) | copy-start | bytes 393220
  7.3 0.9 %copy-start.6 = (bf16[16,4096]{1,0:T(8,128)(2,1)S(1)}, bf16[16,4096]{1,0:T(8,128)(2,1)}, u32[]{:S(2)}) copy-start(bf16[16,4096]{1,0:T(8,128)(2,1)} %adj.1) | copy-start | bytes 393220
  8.2 0.7 %copy-start.7 = (s32[1,4096]{1,0:T(1,128)S(1)}, s32[1,4096]{1,0:T(1,128)}, u32[]{:S(2)}) copy-start(s32[1,4096]{1,0:T(1,128)} %pmap.1) | copy-start | bytes 49156
  8.9 0.7 %copy-start.8 = (s32[1,128]{1,0:T(1,128)S(1)}, s32[1,128]{1,0:T(1,128)}, u32[]{:S(2)}) copy-start(s32[1,128]{1,0:T(1,128)} %slist.1) | copy-start | bytes 1540
  9.5 0.7 %copy-start.9 = (s32[1,128]{1,0:T(1,128)S(1)}, s32[1,128]{1,0:T(1,128)}, u32[]{:S(2)}) copy-start(s32[1,128]{1,0:T(1,128)} %tlist.1) | copy-start | bytes 1540

commit v2 on v1

v2 whole, which is shorter than its diff:
```python
import jax
import jax.numpy as jnp
from jax import lax
from jax.experimental import pallas as pl
from jax.experimental.pallas import tpu as pltpu
from jax.sharding import PartitionSpec as P

F32 = jnp.float32
BF16 = jnp.bfloat16
MESH = pl.DeviceIdType.MESH

FWD = (0, 1, -1, 2, -2, 3, -3, 4)
BWD = (4, 3, -3, 2, -2, 1, -1, 0)
FPOS = {d: i for i, d in enumerate(FWD)}
BPOS = {d: i for i, d in enumerate(BWD)}
FBATCH = ((0, 3), (3, 5), (5, 7), (7, 8))
BBATCH = ((0, 1), (1, 3), (3, 5), (5, 8))


def nt(a, b):
    return lax.dot_general(a, b, (((1,), (1,)), ((), ())), preferred_element_type=F32)


def nn(a, b):
    return lax.dot_general(a, b, (((1,), (0,)), ((), ())), preferred_element_type=F32)


def batch_nt(a, b):
    return lax.dot_general(a, b, (((2,), (2,)), ((0,), (0,))), preferred_element_type=F32)


def batch_nn(a, b):
    return lax.dot_general(a, b, (((2,), (1,)), ((0,), (0,))), preferred_element_type=F32)


def split(a):
    high = a.astype(BF16)
    low = (a - high.astype(F32)).astype(BF16)
    return high, low


def stacked(a):
    high, low = split(a)
    return jnp.concatenate([high, low], axis=0)


def folded(a):
    half = a.shape[0] // 2
    return a[:half] + a[half:]


def xor3(bits, e):
    total = 0
    for i in range(3):
        value = 1 - bits[i] if (e >> i) & 1 else bits[i]
        total = total + value * (1 << i)
    return total


def level_of(e):
    return 0 if e == 1 else (1 if e < 4 else 2)


def kernel(
    inp_h, adj_h, pmap_h, slist_h, tlist_h, bases_h, near_h, trans_h, up_h, down_h, coup_h,
    out_x, out_a,
    inp, adj, pmap, slist, tlist, bases, near, trans, up, down, coup,
    tsm, lsm,
    xl, oh, gath, nx, nw, diff_n, marked,
    ag0, ag1, ag2, ag3, ag4, ag5, ag6, ag7, ws, lists, fsend, frecv, bsend, brecv,
    cws, cwr, ccs, ccr,
    lxs, lxr, lws, lwr, lzs, lzr, lar,
    local_sem, ag_s, ag_r, list_s, list_r, f_s, f_r, b_s, b_r,
    cw_s, cw_r, cc_s, cc_r, lx_s, lx_r, lw_s, lw_r, lz_s, lz_r, la_s, la_r,
):
    ag = (ag0, ag1, ag2, ag3, ag4, ag5, ag6, ag7)
    s = lax.axis_index("sub")
    b = lax.axis_index("blk")

    loads = []

    def load(src, dst):
        copy = pltpu.make_async_copy(src, dst, local_sem.at[len(loads)])
        copy.start()
        loads.append(copy)
        return copy

    early = [load(inp_h, inp), load(adj_h, adj), load(pmap_h, pmap), load(slist_h, slist), load(tlist_h, tlist)]
    bases_in = load(bases_h, bases)
    trans_in = load(trans_h, trans)
    maps_in = [load(up_h, up), load(down_h, down)]
    tsm_in = load(tlist_h, tsm)
    coup_in = load(coup_h, coup)
    near_in = load(near_h, near)

    bits = []
    rest = s
    for _ in range(6):
        half = lax.div(rest, 2)
        bits.append(rest - half * 2)
        rest = half
    w = xor3(bits[:3], 0)
    z = xor3(bits[3:], 0)
    w_at = [xor3(bits[:3], e) for e in range(8)]
    zx_at = [xor3(bits[3:], e) for e in range(8)]
    z_at = {d: lax.rem(z + (d + 8), 8) for d in FWD}
    b_at = [lax.rem(b + d, 4) for d in range(4)]
    z_dev = {d: (z_at[d] * 8 + w, b) for d in FWD}
    zx_dev = [(zx_at[e] * 8 + w, b) for e in range(8)]
    w_dev = [(z * 8 + w_at[e], b) for e in range(8)]
    x_dev = [(s, b_at[d]) for d in range(4)]

    barrier = pltpu.get_barrier_semaphore()
    for e in range(1, 8):
        pl.semaphore_signal(barrier, inc=1, device_id=zx_dev[e], device_id_type=MESH)
        pl.semaphore_signal(barrier, inc=1, device_id=w_dev[e], device_id_type=MESH)
    for d in range(1, 4):
        pl.semaphore_signal(barrier, inc=1, device_id=x_dev[d], device_id_type=MESH)

    def send(src, dst, ssem, rsem, dev):
        copy = pltpu.make_async_remote_copy(
            src_ref=src, dst_ref=dst, send_sem=ssem, recv_sem=rsem, device_id=dev, device_id_type=MESH
        )
        copy.start()
        return copy

    def wait_all(copies):
        for copy in copies:
            copy.wait_recv()

    row = lax.broadcasted_iota(jnp.int32, (256, 256), 0)
    col = lax.broadcasted_iota(jnp.int32, (256, 256), 1)
    diff_n[...] = (row - (col & 15)).astype(F32)
    for copy in early:
        copy.wait()
    for h in range(16):
        xl[h * 32 : h * 32 + 16, :] = inp[:, h * 256 : (h + 1) * 256]
        xl[h * 32 + 16 : h * 32 + 32, :] = adj[:, h * 256 : (h + 1) * 256]
    lists[0] = jnp.broadcast_to(slist[...], (8, 128))

    def leaves_in(step, carry):
        for i in range(4):
            leaf = step * 4 + i
            off = pl.multiple_of(leaf * 256, 256)
            places = pmap[:, pl.ds(off, 256)]
            low, high = places & 255, places >> 8
            hot = jnp.where(lax.broadcasted_iota(jnp.int32, (256, 256), 0) == low, 1.0, 0.0).astype(BF16)
            oh[:, pl.ds(off, 256)] = hot
            every = nn(xl[...], hot)
            vals = jnp.zeros((32, 256), F32)
            for h in range(16):
                vals = vals + jnp.where(high == h, every[h * 32 : (h + 1) * 32, :], 0.0)
            gath[leaf] = vals.astype(BF16)
        return carry

    lax.fori_loop(0, 4, leaves_in, 0)
    bases_in.wait()
    skel = batch_nt(gath[...], bases[...]).astype(BF16)
    ag0[...] = skel[:, :16]
    ws[...] = skel[:, 16:]

    pl.semaphore_wait(barrier, 17)
    cw_in, cc_in = [], []

    def ag_cw(k):
        dst = 4 if k == 3 else -(k + 1)
        cw_in.append(send(ag[FPOS[-k]], ag[FPOS[dst]], ag_s.at[k], ag_r.at[k], z_dev[1]))

    def ag_cc(k):
        cc_in.append(send(ag[FPOS[k]], ag[FPOS[k + 1]], ag_s.at[4 + k], ag_r.at[4 + k], z_dev[-1]))

    ag_cw(0)
    ag_cc(0)
    list_in = []
    for i, d in enumerate((1, -1, 2, -2, 3, -3, 4)):
        origin = 4 if d == 4 else -d
        list_in.append(send(lists.at[0], lists.at[FPOS[origin]], list_s.at[i], list_r.at[i], z_dev[d]))

    trans_in.wait()
    xd = jnp.zeros((16, 128), F32)
    wd = jnp.zeros((16, 128), F32)
    for leaf in range(16):
        xd = xd + nt(skel[leaf, :16], trans[leaf])
        wd = wd + nn(skel[leaf, 16:], trans[leaf])
    for copy in maps_in:
        copy.wait()
    xd2, wd2 = stacked(xd), stacked(wd)
    for v in range(6):
        cx = folded(nt(xd2, up[v]))
        cw = folded(nn(wd2, down[v]))
        lxs[0, v] = cx[:8]
        lxs[1, v] = cx[8:]
        lxs[2, v] = cw[:8]
        lxs[3, v] = cw[8:]
    lx_in = [
        send(lxs.at[b_at[d]], lxr.at[d - 1], lx_s.at[d - 1], lx_r.at[d - 1], x_dev[d]) for d in range(1, 4)
    ]

    f_in, b_in = [], []

    def plane_send(buf_s, buf_r, lo, hi, sems_s, sems_r, k):
        copies = []
        for e in range(1, 8):
            copies.append(
                send(
                    buf_s.at[w_at[e], pl.ds(lo, hi - lo)],
                    buf_r.at[w, pl.ds(lo, hi - lo)],
                    sems_s.at[k, e - 1],
                    sems_r.at[k, e - 1],
                    w_dev[e],
                )
            )
        buf_r[w, lo:hi] = buf_s[w, lo:hi]
        return copies

    tsm_in.wait()
    coup_in.wait()

    def b_batch(k):
        lo, hi = BBATCH[k]
        for pos in range(lo, hi):
            first = z_at[BWD[pos]] * 16
            for i in range(16):
                ret = nn(ws[tsm[0, first + i]], coup[first + i]).astype(BF16)
                bsend[i // 2, pos, (i % 2) * 16 : (i % 2) * 16 + 16] = ret
        b_in.append(plane_send(bsend, brecv, lo, hi, b_s, b_r, k))

    b_batch(0)
    b_batch(1)

    lane = lax.broadcasted_iota(jnp.int32, (8, 128), 1)
    spread = (
        (lax.broadcasted_iota(jnp.int32, (128, 256), 0) & 15) == (lax.broadcasted_iota(jnp.int32, (128, 256), 1) >> 4)
    ).astype(F32).astype(BF16)
    turn = (lax.broadcasted_iota(jnp.int32, (8, 128), 0) + z) & 7
    t_rows = jnp.broadcast_to(tlist[...], (8, 128))
    t_line = nn(jnp.where((lane >> 4) == turn, t_rows * 16, 0).astype(F32).astype(BF16), spread)

    def sum_matrix(line):
        return jnp.where(diff_n[...] == line, 1.0, 0.0).astype(BF16)

    def select(pos):
        for i in range(16):
            leaf = lsm[pos, 0, z * 16 + i]
            fsend[i // 2, pos, (i % 2) * 16 : (i % 2) * 16 + 16] = ag[pos][leaf]

    def f_batch(k):
        lo, hi = FBATCH[k]
        for pos in range(lo, hi):
            select(pos)
        f_in.append(plane_send(fsend, frecv, lo, hi, f_s, f_r, k))

    rs_cw, rs_cc = [], []

    def rs_cw_send(k, value):
        cws[k] = value.astype(BF16)
        rs_cw.append(send(cws.at[k], cwr.at[k], cw_s.at[k], cw_r.at[k], z_dev[1]))

    def rs_cc_send(k, value):
        ccs[k] = value.astype(BF16)
        rs_cc.append(send(ccs.at[k], ccr.at[k], cc_s.at[k], cc_r.at[k], z_dev[-1]))

    def list_chunk(pos, total):
        delta = FWD[pos]
        inc = frecv[:, pos].reshape(16, 16, 128)
        mats = coup[pl.ds(pl.multiple_of(z_at[delta] * 16, 16), 16)]
        terms = batch_nt(inc, mats).reshape(256, 128)
        high, low = split(terms)
        r = delta % 8
        both = nn(sum_matrix(t_line[r : r + 1]), jnp.concatenate([high, low], axis=1))
        return total + both[:, :128] + both[:, 128:]

    cw_in[0].wait_recv()
    ag_cw(1)
    cc_in[0].wait_recv()
    ag_cc(1)
    wait_all(list_in)
    lists_in = load(lists, lsm)
    b_batch(2)

    l_line = nn(
        jnp.where((lane >> 4) == z, lists[:, 0, :] * 16, 0).astype(F32).astype(BF16), spread
    )

    def part(delta):
        pos = FPOS[delta]
        return nn(sum_matrix(l_line[pos : pos + 1]), brecv[:, BPOS[delta]].reshape(256, 128))

    wait_all(lx_in)
    mine = lxs[b] + lxr[0] + lxr[1] + lxr[2]
    for v in range(3):
        lws[v, 0] = mine[v]
        lws[v, 1:4] = mine[3:6]
    lw_in = [
        send(lws.at[level_of(e)], lwr.at[e - 1], lw_s.at[e - 1], lw_r.at[e - 1], w_dev[e]) for e in range(1, 8)
    ]

    lists_in.wait()
    f_batch(0)
    b_batch(3)

    wait_all(b_in[0])
    rs_cc_send(0, part(4))
    wait_all(b_in[1])
    rs_cw_send(0, part(3))
    here_m3 = part(-3)

    near_in.wait()
    nx[...] = batch_nt(gath[:, :16], near[...])

    cw_in[1].wait_recv()
    ag_cw(2)
    cc_in[1].wait_recv()
    ag_cc(2)
    f_batch(1)

    wait_all(lw_in)
    upper = mine[3:6]
    for e in range(1, 8):
        upper = upper + lwr[e - 1, 1:4]
    for v in range(3):
        lzs[v] = upper[v]
    lz_in = [send(lzs.at[level_of(e)], lzr.at[e - 1], lz_s.at[e - 1], lz_r.at[e - 1], zx_dev[e]) for e in range(1, 8)]

    wait_all(b_in[2])
    here_p, here_m = part(2), part(-2)
    rs_cc[0].wait_recv()
    rs_cc_send(1, here_m3 + ccr[0].astype(F32))
    rs_cw[0].wait_recv()
    rs_cw_send(1, here_p + cwr[0].astype(F32))

    nw[...] = batch_nn(gath[:, 16:], near[...])

    cw_in[2].wait_recv()
    ag_cw(3)
    cc_in[2].wait_recv()
    f_batch(2)

    wait_all(lz_in)
    quarter = [
        lwr[0, 0],
        lwr[1, 0] + lwr[2, 0],
        lwr[3, 0] + lwr[4, 0] + lwr[5, 0] + lwr[6, 0],
        lzr[0],
        lzr[1] + lzr[2],
        lzr[3] + lzr[4] + lzr[5] + lzr[6],
    ]
    for v in range(6):
        lar[b, v] = quarter[v]
    la_in = [send(lar.at[b], lar.at[b], la_s.at[d - 1], la_r.at[d - 1], x_dev[d]) for d in range(1, 4)]

    wait_all(b_in[3])
    here_p1, here_m1, own = part(1), part(-1), part(0)
    rs_cc[1].wait_recv()
    rs_cc_send(2, here_m + ccr[1].astype(F32))
    rs_cw[1].wait_recv()
    rs_cw_send(2, here_p1 + cwr[1].astype(F32))

    wait_all(f_in[0])
    lx = jnp.zeros((256, 128), F32)
    for pos in range(0, 3):
        lx = list_chunk(pos, lx)

    cw_in[3].wait_recv()
    f_batch(3)

    wait_all(la_in)
    yd = jnp.zeros((32, 128), F32)
    zd = jnp.zeros((32, 128), F32)
    for v in range(6):
        sx = jnp.concatenate([lar[0, v], lar[1, v]], axis=0)
        sw = jnp.concatenate([lar[2, v], lar[3, v]], axis=0)
        yd = yd + nt(stacked(sx), down[v])
        zd = zd + nn(stacked(sw), up[v])
    yd2, zd2 = stacked(folded(yd)), stacked(folded(zd))

    wait_all(f_in[1])
    for pos in range(3, 5):
        lx = list_chunk(pos, lx)

    rs_cc[2].wait_recv()
    rs_cc_send(3, here_m1 + ccr[2].astype(F32))

    wait_all(f_in[2])
    for pos in range(5, 7):
        lx = list_chunk(pos, lx)

    def expansions(value, from_lists, dot):
        rows = [folded(dot(value, trans[leaf])) for leaf in range(16)]
        return jnp.stack(rows, axis=0) + from_lists.reshape(16, 16, 128)

    def place(exp, near_term, out):
        vals = (batch_nn(exp.astype(BF16), bases[...]) + near_term[...]).astype(BF16).astype(F32)
        for leaf in range(16):
            high = pmap[:, leaf * 256 : (leaf + 1) * 256] >> 8
            marked[:, leaf * 256 : (leaf + 1) * 256] = jnp.concatenate(
                [jnp.where(high == h, vals[leaf], 0.0) for h in range(16)], axis=0
            ).astype(BF16)
        res = nt(marked[...], oh[...]).astype(BF16)
        for h in range(16):
            out[:, h * 256 : (h + 1) * 256] = res[h * 16 : h * 16 + 16]

    wait_all(f_in[3])
    lx = list_chunk(7, lx)
    place(expansions(yd2, lx, nn), nx, out_x)

    rs_cw[2].wait_recv()
    rs_cc[3].wait_recv()
    lw = own + cwr[2].astype(F32) + ccr[3].astype(F32)
    place(expansions(zd2, lw, nt), nw, out_a)

    for copies in [list_in, cw_in, cc_in, lx_in, lw_in, lz_in, la_in, rs_cw, rs_cc] + f_in + b_in:
        for copy in copies:
            copy.wait_send()


def hand_over(x_ref, a_ref, out_x, out_a):
    out_x[...] = x_ref[...]
    out_a[...] = a_ref[...]


def shards(inputs, adjoint_in, panel_map, bases, near, trans, up, down, send_list, target_leaf, coup):
    vmem = pl.BlockSpec(memory_space=pltpu.VMEM)
    hbm = pl.BlockSpec(memory_space=pltpu.HBM)
    dma = pltpu.SemaphoreType.DMA
    both = pl.pallas_call(
        kernel,
        out_shape=(jax.ShapeDtypeStruct((16, 4096), BF16), jax.ShapeDtypeStruct((16, 4096), BF16)),
        in_specs=[hbm] * 11,
        out_specs=(vmem, vmem),
        scratch_shapes=[
            pltpu.VMEM((16, 4096), BF16),
            pltpu.VMEM((16, 4096), BF16),
            pltpu.VMEM((1, 4096), jnp.int32),
            pltpu.VMEM((1, 128), jnp.int32),
            pltpu.VMEM((1, 128), jnp.int32),
            pltpu.VMEM((16, 128, 256), BF16),
            pltpu.VMEM((16, 256, 256), BF16),
            pltpu.VMEM((16, 128, 128), BF16),
            pltpu.VMEM((6, 128, 128), BF16),
            pltpu.VMEM((6, 128, 128), BF16),
            pltpu.VMEM((128, 128, 128), BF16),
            pltpu.SMEM((1, 128), jnp.int32),
            pltpu.SMEM((8, 8, 128), jnp.int32),
            pltpu.VMEM((512, 256), BF16),
            pltpu.VMEM((256, 4096), BF16),
            pltpu.VMEM((16, 32, 256), BF16),
            pltpu.VMEM((16, 16, 256), F32),
            pltpu.VMEM((16, 16, 256), F32),
            pltpu.VMEM((256, 256), F32),
            pltpu.VMEM((256, 4096), BF16),
        ]
        + [pltpu.VMEM((16, 16, 128), BF16)] * 8
        + [
            pltpu.VMEM((16, 16, 128), BF16),
            pltpu.VMEM((8, 8, 128), jnp.int32),
            pltpu.VMEM((8, 8, 32, 128), BF16),
            pltpu.VMEM((8, 8, 32, 128), BF16),
            pltpu.VMEM((8, 8, 32, 128), BF16),
            pltpu.VMEM((8, 8, 32, 128), BF16),
            pltpu.VMEM((3, 256, 128), BF16),
            pltpu.VMEM((3, 256, 128), BF16),
            pltpu.VMEM((4, 256, 128), BF16),
            pltpu.VMEM((4, 256, 128), BF16),
            pltpu.VMEM((4, 6, 8, 128), F32),
            pltpu.VMEM((3, 6, 8, 128), F32),
            pltpu.VMEM((3, 4, 8, 128), F32),
            pltpu.VMEM((7, 4, 8, 128), F32),
            pltpu.VMEM((3, 8, 128), F32),
            pltpu.VMEM((7, 8, 128), F32),
            pltpu.VMEM((4, 6, 8, 128), F32),
            dma((13,)),
            dma((7,)), dma((7,)),
            dma((7,)), dma((7,)),
            dma((4, 7)), dma((4, 7)),
            dma((4, 7)), dma((4, 7)),
            dma((3,)), dma((3,)),
            dma((4,)), dma((4,)),
            dma((3,)), dma((3,)),
            dma((7,)), dma((7,)),
            dma((7,)), dma((7,)),
            dma((3,)), dma((3,)),
        ],
        compiler_params=pltpu.CompilerParams(
            collective_id=0, has_side_effects=True, vmem_limit_bytes=60 * 1024 * 1024
        ),
    )(inputs, adjoint_in, panel_map, send_list, target_leaf, bases, near, trans, up, down, coup)
    shape = jax.ShapeDtypeStruct((16, 4096), BF16)
    return pl.pallas_call(hand_over, out_shape=(shape, shape), in_specs=[vmem] * 2, out_specs=(vmem, vmem))(*both)


def solution(mesh):
    each = ("sub", "blk")
    return jax.shard_map(
        shards,
        mesh=mesh,
        in_specs=(
            P(None, each),
            P(None, each),
            P(each, None),
            P(each, None, None),
            P(each, None, None),
            P(each, None, None),
            P(each, None, None),
            P(each, None, None),
            P(each, None),
            P(each, None),
            P(each, None, None),
        ),
        out_specs=(P(None, each), P(None, each)),
        check_vma=False,
    )
```

time: 58.9 us -> 42.3 us (0.72)
  local copies, waits for them, and re-layouts: 10.8 us -> 0 us
  Pallas kernels: 47 us -> 41.6 us
    unnamed x22 -> x0, local copies, waits for them, and re-layouts: 10.8 us -> none
    pallas_call x1, Pallas kernels: 47 us -> 39.9 us  [shards(): pl.pallas_call(kernel, out_shape=(jax.ShapeDtypeStruct((16, 4096), BF16),...]
    pallas_call x0 -> x1, Pallas kernels: none -> 1.68 us  [shards(): pl.pallas_call(hand_over, out_shape=(shape, shape), in_specs=[vmem] * 2,...]
where the time goes in v2:
time: 42.3 us; the launch traced here: 42.2 us
  Pallas kernels  41.6 us (98%)
  between operations  0.64 us (2%)
    pallas_call x1, Pallas kernels, shards(): pl.pallas_call(kernel, out_shape=(jax.ShapeDtypeStruct((16, 4096), BF16),...  39.9 us
    pallas_call x1, Pallas kernels, shards(): pl.pallas_call(hand_over, out_shape=(shape, shape), in_specs=[vmem] * 2,...  1.68 us

profile of v2, /device:TPU:1, one launch (start us, length us, event | category | flops | bytes accessed | tf_op | source)
XLA Modules:
  0.0 42.2 jit_solution(12569160078009588207)
XLA Ops:
  0.6 39.9 %shard_map.122 = (bf16[16,4096]{1,0:T(8,128)(2,1)}, bf16[16,4096]{1,0:T(8,128)(2,1)}) custom-call(bf16[16,4096]{1,0:T(8,128)(2,1)} %inp_h.1, bf16[16,4096]{1,0:T(8,128)(2,1)} %adj_h.1, s32[1,4096]{1,0:T(1,128)} %pmap_h.1, s32[1,128]{1,0:T(1,128)} %slist_h.1, s32[1,128]{1,0:T(1,128)} %tlist_h.1, bf16[16,128,256]{2,1,0:T(8,128)(2,1)} %bases_h.1, ...), custom_call_target="tpu_custom_call" | custom-call | tf_op jit(solution)/shard_map/pallas_call | solution.py:426
  40.5 1.7 %shard_map.123 = (bf16[16,4096]{1,0:T(8,128)(2,1)}, bf16[16,4096]{1,0:T(8,128)(2,1)}) custom-call(bf16[16,4096]{1,0:T(8,128)(2,1)} %get-tuple-element.4.x_ref, bf16[16,4096]{1,0:T(8,128)(2,1)} %get-tuple-element.5.a_ref), custom_call_target="tpu_custom_call" | custom-call | tf_op jit(solution)/shard_map/pallas_call | solution.py:489

commit v3 on v2

--- a/solution.py
+++ b/solution.py
@@ -13,7 +13,7 @@
 BWD = (4, 3, -3, 2, -2, 1, -1, 0)
 FPOS = {d: i for i, d in enumerate(FWD)}
 BPOS = {d: i for i, d in enumerate(BWD)}
-FBATCH = ((0, 3), (3, 5), (5, 7), (7, 8))
+FBATCH = ((0, 3), (3, 7), (7, 8))
 BBATCH = ((0, 1), (1, 3), (3, 5), (5, 8))
 
 
@@ -66,7 +66,7 @@
     out_x, out_a,
     inp, adj, pmap, slist, tlist, bases, near, trans, up, down, coup,
     tsm, lsm,
-    xl, oh, gath, nx, nw, diff_n, marked,
+    xl, oh, oh_t, gath, nx, nw, diff_n, marked,
     ag0, ag1, ag2, ag3, ag4, ag5, ag6, ag7, ws, lists, fsend, frecv, bsend, brecv,
     cws, cwr, ccs, ccr,
     lxs, lxr, lws, lwr, lzs, lzr, lar,
@@ -312,7 +312,6 @@
     ag_cw(2)
     cc_in[1].wait_recv()
     ag_cc(2)
-    f_batch(1)
 
     wait_all(lw_in)
     upper = mine[3:6]
@@ -330,11 +329,16 @@
     rs_cw_send(1, here_p + cwr[0].astype(F32))
 
     nw[...] = batch_nn(gath[:, 16:], near[...])
+    unit = jnp.where(row == col, 1.0, 0.0).astype(BF16)
+    for leaf in range(16):
+        oh_t[leaf * 256 : (leaf + 1) * 256, :] = lax.dot_general(
+            oh[:, leaf * 256 : (leaf + 1) * 256], unit, (((0,), (0,)), ((), ())), preferred_element_type=F32
+        ).astype(BF16)
 
     cw_in[2].wait_recv()
     ag_cw(3)
     cc_in[2].wait_recv()
-    f_batch(2)
+    f_batch(1)
 
     wait_all(lz_in)
     quarter = [
@@ -362,7 +366,7 @@
         lx = list_chunk(pos, lx)
 
     cw_in[3].wait_recv()
-    f_batch(3)
+    f_batch(2)
 
     wait_all(la_in)
     yd = jnp.zeros((32, 128), F32)
@@ -373,6 +377,8 @@
         yd = yd + nt(stacked(sx), down[v])
         zd = zd + nn(stacked(sw), up[v])
     yd2, zd2 = stacked(folded(yd)), stacked(folded(zd))
+    y_leaf = jnp.stack([folded(nn(yd2, trans[leaf])) for leaf in range(16)], axis=0)
+    z_leaf = jnp.stack([folded(nt(zd2, trans[leaf])) for leaf in range(16)], axis=0)
 
     wait_all(f_in[1])
     for pos in range(3, 5):
@@ -381,13 +387,8 @@
     rs_cc[2].wait_recv()
     rs_cc_send(3, here_m1 + ccr[2].astype(F32))
 
-    wait_all(f_in[2])
     for pos in range(5, 7):
         lx = list_chunk(pos, lx)
-
-    def expansions(value, from_lists, dot):
-        rows = [folded(dot(value, trans[leaf])) for leaf in range(16)]
-        return jnp.stack(rows, axis=0) + from_lists.reshape(16, 16, 128)
 
     def place(exp, near_term, out):
         vals = (batch_nn(exp.astype(BF16), bases[...]) + near_term[...]).astype(BF16).astype(F32)
@@ -396,18 +397,18 @@
             marked[:, leaf * 256 : (leaf + 1) * 256] = jnp.concatenate(
                 [jnp.where(high == h, vals[leaf], 0.0) for h in range(16)], axis=0
             ).astype(BF16)
-        res = nt(marked[...], oh[...]).astype(BF16)
+        res = nn(marked[...], oh_t[...]).astype(BF16)
         for h in range(16):
             out[:, h * 256 : (h + 1) * 256] = res[h * 16 : h * 16 + 16]
 
-    wait_all(f_in[3])
+    wait_all(f_in[2])
     lx = list_chunk(7, lx)
-    place(expansions(yd2, lx, nn), nx, out_x)
+    place(y_leaf + lx.reshape(16, 16, 128), nx, out_x)
 
     rs_cw[2].wait_recv()
     rs_cc[3].wait_recv()
     lw = own + cwr[2].astype(F32) + ccr[3].astype(F32)
-    place(expansions(zd2, lw, nt), nw, out_a)
+    place(z_leaf + lw.reshape(16, 16, 128), nw, out_a)
 
     for copies in [list_in, cw_in, cc_in, lx_in, lw_in, lz_in, la_in, rs_cw, rs_cc] + f_in + b_in:
         for copy in copies:
@@ -444,6 +445,7 @@
             pltpu.SMEM((8, 8, 128), jnp.int32),
             pltpu.VMEM((512, 256), BF16),
             pltpu.VMEM((256, 4096), BF16),
+            pltpu.VMEM((4096, 256), BF16),
             pltpu.VMEM((16, 32, 256), BF16),
             pltpu.VMEM((16, 16, 256), F32),
             pltpu.VMEM((16, 16, 256), F32),

time: 42.3 us -> 41.9 us (level)
  Pallas kernels: 41.6 us -> 41.1 us
    pallas_call x1, Pallas kernels: 39.9 us -> 39.4 us  [shards(): pl.pallas_call(kernel, out_shape=(jax.ShapeDtypeStruct((16, 4096), BF16),...]
where the time goes in v3:
time: 41.9 us; the launch traced here: 41.7 us
  Pallas kernels  41.1 us (98%)
  between operations  0.64 us (2%)
    pallas_call x1, Pallas kernels, shards(): pl.pallas_call(kernel, out_shape=(jax.ShapeDtypeStruct((16, 4096), BF16),...  39.4 us
    pallas_call x1, Pallas kernels, shards(): pl.pallas_call(hand_over, out_shape=(shape, shape), in_specs=[vmem] * 2,...  1.68 us

profile of v3, /device:TPU:1, one launch (start us, length us, event | category | flops | bytes accessed | tf_op | source)
XLA Modules:
  0.0 41.7 jit_solution(1970544397909487748)
XLA Ops:
  0.6 39.4 %shard_map.122 = (bf16[16,4096]{1,0:T(8,128)(2,1)}, bf16[16,4096]{1,0:T(8,128)(2,1)}) custom-call(bf16[16,4096]{1,0:T(8,128)(2,1)} %inp_h.1, bf16[16,4096]{1,0:T(8,128)(2,1)} %adj_h.1, s32[1,4096]{1,0:T(1,128)} %pmap_h.1, s32[1,128]{1,0:T(1,128)} %slist_h.1, s32[1,128]{1,0:T(1,128)} %tlist_h.1, bf16[16,128,256]{2,1,0:T(8,128)(2,1)} %bases_h.1, ...), custom_call_target="tpu_custom_call" | custom-call | tf_op jit(solution)/shard_map/pallas_call | solution.py:427
  40.0 1.7 %shard_map.123 = (bf16[16,4096]{1,0:T(8,128)(2,1)}, bf16[16,4096]{1,0:T(8,128)(2,1)}) custom-call(bf16[16,4096]{1,0:T(8,128)(2,1)} %get-tuple-element.4.x_ref, bf16[16,4096]{1,0:T(8,128)(2,1)} %get-tuple-element.5.a_ref), custom_call_target="tpu_custom_call" | custom-call | tf_op jit(solution)/shard_map/pallas_call | solution.py:491

commit v4 on v3

--- a/solution.py
+++ b/solution.py
@@ -90,8 +90,6 @@
     trans_in = load(trans_h, trans)
     maps_in = [load(up_h, up), load(down_h, down)]
     tsm_in = load(tlist_h, tsm)
-    coup_in = load(coup_h, coup)
-    near_in = load(near_h, near)
 
     bits = []
     rest = s
@@ -133,6 +131,8 @@
     diff_n[...] = (row - (col & 15)).astype(F32)
     for copy in early:
         copy.wait()
+    coup_in = load(coup_h, coup)
+    near_in = load(near_h, near)
     for h in range(16):
         xl[h * 32 : h * 32 + 16, :] = inp[:, h * 256 : (h + 1) * 256]
         xl[h * 32 + 16 : h * 32 + 32, :] = adj[:, h * 256 : (h + 1) * 256]

time: 41.9 us -> 41.9 us (level)
  no operation moved by 1% of the time
where the time goes in v4:
time: 41.9 us; the launch traced here: 41.7 us
  Pallas kernels  41.1 us (98%)
  between operations  0.64 us (2%)
    pallas_call x1, Pallas kernels, shards(): pl.pallas_call(kernel, out_shape=(jax.ShapeDtypeStruct((16, 4096), BF16),...  39.4 us
    pallas_call x1, Pallas kernels, shards(): pl.pallas_call(hand_over, out_shape=(shape, shape), in_specs=[vmem] * 2,...  1.68 us

profile of v4, /device:TPU:1, one launch (start us, length us, event | category | flops | bytes accessed | tf_op | source)
XLA Modules:
  0.0 41.7 jit_solution(10918674562853194137)
XLA Ops:
  0.6 39.4 %shard_map.122 = (bf16[16,4096]{1,0:T(8,128)(2,1)}, bf16[16,4096]{1,0:T(8,128)(2,1)}) custom-call(bf16[16,4096]{1,0:T(8,128)(2,1)} %inp_h.1, bf16[16,4096]{1,0:T(8,128)(2,1)} %adj_h.1, s32[1,4096]{1,0:T(1,128)} %pmap_h.1, s32[1,128]{1,0:T(1,128)} %slist_h.1, s32[1,128]{1,0:T(1,128)} %tlist_h.1, bf16[16,128,256]{2,1,0:T(8,128)(2,1)} %bases_h.1, ...), custom_call_target="tpu_custom_call" | custom-call | tf_op jit(solution)/shard_map/pallas_call | solution.py:427
  40.0 1.7 %shard_map.123 = (bf16[16,4096]{1,0:T(8,128)(2,1)}, bf16[16,4096]{1,0:T(8,128)(2,1)}) custom-call(bf16[16,4096]{1,0:T(8,128)(2,1)} %get-tuple-element.4.x_ref, bf16[16,4096]{1,0:T(8,128)(2,1)} %get-tuple-element.5.a_ref), custom_call_target="tpu_custom_call" | custom-call | tf_op jit(solution)/shard_map/pallas_call | solution.py:491
